TPU v7x, 128 devices: a whole 4x4x4 slice. The times are simulated.
128 devices in a mesh: cfg: 2 (over z_lo), seq: 8 (over x, core), head: 8 (over y, z_hi).
Axes of the slice: x: 4, y: 4, z: 4 (z_hi: 2, z_lo: 2; z = z_hi * 2 + z_lo), core: 2. Of those that a mesh axis runs over, the one named last changes fastest.
Arguments:
- q_img: bfloat16 [2, 8192, 2560], P('cfg', ('seq', 'head')), may hold values from -240 to 240
- k_img: bfloat16 [2, 8192, 2560], P('cfg', ('seq', 'head')), may hold values from -6 to 6
- v_img: bfloat16 [2, 8192, 2560], P('cfg', ('seq', 'head')), may hold values from -6 to 6
- text_k: bfloat16 [2, 384, 2560], P('cfg'), may hold values from -6 to 6
- text_v: bfloat16 [2, 384, 2560], P('cfg'), may hold values from -6 to 6
- text_len: int32 [2], P('cfg'), may hold values from 1 to 384, as said below
- head_mask: int32 [40], replicated, may hold values 0 or 1
- hidden: bfloat16 [2, 8192, 2432], P('cfg', ('seq', 'head')), may hold values from -6 to 6
- out_weight: bfloat16 [2560, 2432], P('head'), may hold values from -0.125 to 0.125
- out_bias: bfloat16 [2432], replicated, may hold values from -3 to 3
- final_shift: bfloat16 [2, 2432], P('cfg'), may hold values from -3 to 3
- final_scale: bfloat16 [2, 2432], P('cfg'), may hold values from -1.5 to 1.5
- final_weight: bfloat16 [64, 2432], replicated, may hold values from -0.125 to 0.125
- latent: float32 [64, 8192], P('cfg', ('seq', 'head')), may hold values from -6 to 6
- step_index: int32 [1], replicated, may hold values from 0 to 27
Outputs:
- next_latent: float32 [64, 8192], P('cfg', ('seq', 'head'))
- denoised: float32 [64, 8192], P('cfg', ('seq', 'head'))
Inputs may be any that keep to these rules, and one draw needn't show every extreme that they name: `text_len`: some branch has all 384 text tokens live.
All inputs are finite; a program needn't handle non-finite values.
Results may differ from a plain program's by a relative error of at most 0.0085.
Values may be sent and summed in bfloat16 or wider, within the bound.
A program may use at most 128 MiB of HBM per device.

v0:
```python
import functools

import jax
import jax.numpy as jnp
from jax import lax
from jax.experimental import pallas as pl
from jax.experimental.pallas import tpu as pltpu
from jax.sharding import PartitionSpec as P

HDIM = 64
STEPS = 28
GUIDANCE = 3.5
GROUP_HEADS = 5
FEATURES = 320
TOKENS = 128
SLOTS = 384
QUERIES = 1024
TILE = 256
SCORE_SCALE = 0.125 * 1.4426950408889634
MESH = pl.DeviceIdType.MESH
f32 = jnp.float32
bf16 = jnp.bfloat16


def sigma_at(position):
    level = 1.0 - position.astype(jnp.float32) / STEPS
    return 3.0 * level / (1.0 + 2.0 * level)


def attention_kernel(
    q_hbm,
    k_hbm,
    v_hbm,
    tk_hbm,
    tv_hbm,
    bias_ref,
    mask_ref,
    o_ref,
    loaded,
    text_slab,
    q_stage,
    kv_stage,
    o_stage,
    q_recv,
    kv,
    qx,
    text_keys,
    text_values,
    s0,
    s1,
    p0,
    p1,
    m_ref,
    acc,
    load_sem,
    q_send,
    q_recv_sem,
    a_send,
    a_recv,
    b_send,
    b_recv,
    o_send,
    o_recv,
):
    seq = lax.axis_index("seq")
    group = lax.axis_index("head")
    core = lax.rem(seq, 2)
    parity = lax.rem(group, 2)
    right = lax.rem(seq + 2, 8)
    left = lax.rem(seq + 6, 8)
    sibling = seq + 1 - 2 * core
    far = lax.rem(seq + 2 + 4 * core, 8)

    slab_start = pl.multiple_of(128 * ((5 * group) // 2), 128)
    loads = [
        pltpu.make_async_copy(src.at[0], loaded.at[i], load_sem.at[i])
        for i, src in enumerate((q_hbm, k_hbm, v_hbm))
    ] + [
        pltpu.make_async_copy(
            src.at[0, :, pl.ds(slab_start, 384)], text_slab.at[i], load_sem.at[3 + i]
        )
        for i, src in enumerate((tk_hbm, tv_hbm))
    ]
    for load in loads:
        load.start()

    barrier = pltpu.get_barrier_semaphore()
    for d in range(1, 8):
        pl.semaphore_signal(
            barrier, inc=1, device_id={"head": lax.rem(group + d, 8)}, device_id_type=MESH
        )
    for near in (right, left, sibling):
        pl.semaphore_signal(barrier, inc=1, device_id={"seq": near}, device_id_type=MESH)

    low = lax.broadcasted_iota(jnp.int32, (TOKENS, 128), 1) < HDIM
    low_half = lax.broadcasted_iota(jnp.int32, (HDIM, 128), 1) < HDIM

    loads[0].wait()
    for i in range(20):
        block = loaded[0, :, 128 * i : 128 * (i + 1)].T
        for half in range(2):
            f = 128 * i + HDIM * half
            q_stage[f // FEATURES, pl.ds(f % FEATURES, HDIM), :] = block[HDIM * half : HDIM * (half + 1)]
    pl.semaphore_wait(barrier, 10)

    def q_copy(d):
        peer = lax.rem(group + d, 8)
        return pltpu.make_async_remote_copy(
            src_ref=q_stage.at[peer],
            dst_ref=q_recv.at[group],
            send_sem=q_send.at[d],
            recv_sem=q_recv_sem.at[d],
            device_id={"head": peer},
            device_id_type=MESH,
        )

    def kv_copy(d):
        peer = lax.rem(group + d, 8)
        return pltpu.make_async_remote_copy(
            src_ref=kv_stage.at[peer],
            dst_ref=kv.at[d % 2, group // 2],
            send_sem=a_send.at[d],
            recv_sem=a_recv.at[d],
            device_id={"head": peer},
            device_id_type=MESH,
        )

    order = (2, 6, 4, 1, 7, 3, 5)
    for d in order:
        q_copy(d).start()
    q_recv[pl.ds(group, 1)] = q_stage[pl.ds(group, 1)]

    loads[1].wait()
    loads[2].wait()
    for p in range(8):
        first = (5 * p) // 2
        tiles = [
            loaded[1, :, 128 * (first + i) : 128 * (first + i + 1)].astype(f32) for i in range(3)
        ]
        if p % 2 == 0:
            kv_stage[p, 0:128, :] = tiles[0].astype(bf16)
            kv_stage[p, 128:256, :] = tiles[1].astype(bf16)
            last = jnp.where(low_half, tiles[2][:HDIM], pltpu.roll(tiles[2][HDIM:], HDIM, 1))
        else:
            kv_stage[p, 0:128, :] = jnp.where(low, tiles[1], tiles[0]).astype(bf16)
            kv_stage[p, 128:256, :] = jnp.where(low, tiles[2], tiles[1]).astype(bf16)
            last = jnp.where(low_half, pltpu.roll(tiles[2][:HDIM], HDIM, 1), tiles[2][HDIM:])
        kv_stage[p, 256:320, :] = last.astype(bf16)
    for i in range(20):
        block = loaded[2, :, 128 * i : 128 * (i + 1)].T
        for half in range(2):
            f = 128 * i + HDIM * half
            kv_stage[f // FEATURES, pl.ds(FEATURES + f % FEATURES, HDIM), :] = block[
                HDIM * half : HDIM * (half + 1)
            ]
    for d in order:
        kv_copy(d).start()
    kv[0, pl.ds(group // 2, 1)] = kv_stage[pl.ds(group, 1)]

    loads[3].wait()
    loads[4].wait()
    odd = parity == 1
    swap = jnp.logical_and(lax.broadcasted_iota(jnp.int32, (SLOTS, 128), 1) < HDIM, odd)
    slabs = [text_slab[0, :, 128 * i : 128 * (i + 1)].astype(f32) for i in range(3)]
    text_keys[0] = jnp.where(swap, slabs[1], slabs[0]).astype(bf16)
    text_keys[1] = jnp.where(swap, slabs[2], slabs[1]).astype(bf16)
    text_keys[2] = slabs[2].astype(bf16)
    for i in range(3):
        for j in range(3):
            text_values[128 * i : 128 * (i + 1), 128 * j : 128 * (j + 1)] = text_slab[
                1, 128 * j : 128 * (j + 1), 128 * i : 128 * (i + 1)
            ].T

    for d in order:
        q_copy(d).wait_recv()
    zero = jnp.zeros((HDIM, TILE), bf16)

    def place(t, _):
        for h in range(GROUP_HEADS):
            q = jnp.concatenate(
                [q_recv[2 * t, HDIM * h : HDIM * (h + 1)], q_recv[2 * t + 1, HDIM * h : HDIM * (h + 1)]], 1
            )
            if h < 4:
                offset = parity if h % 2 == 0 else 1 - parity
                qx[6 * t + h, pl.ds(pl.multiple_of(HDIM * offset, HDIM), HDIM), :] = q
                qx[6 * t + h, pl.ds(pl.multiple_of(HDIM * (1 - offset), HDIM), HDIM), :] = zero
            else:
                for side in range(2):
                    qx[6 * t + 4 + side, HDIM * side : HDIM * (side + 1), :] = q
                    qx[6 * t + 4 + side, HDIM * (1 - side) : HDIM * (2 - side), :] = zero
        return 0

    lax.fori_loop(0, 4, place, 0)

    ones = jnp.ones((16, 512), bf16)

    def text_units(t, _):
        for h in range(GROUP_HEADS):
            weights_at = 6 * t + h if h < 4 else 6 * t + 4 + parity
            s = jnp.dot(text_keys[h // 2], qx[weights_at], preferred_element_type=f32) + bias_ref[...]
            top = jnp.max(s, axis=0, keepdims=True)
            p = jnp.exp2((s - top) * SCORE_SCALE).astype(bf16)
            values = text_values[pl.ds(pl.multiple_of(HDIM * (parity + h), HDIM), HDIM), :]
            acc[GROUP_HEADS * t + h] = jnp.dot(
                jnp.concatenate([values, ones[:, :SLOTS]], 0), p, preferred_element_type=f32
            )
            m_ref[GROUP_HEADS * t + h] = top
        return 0

    lax.fori_loop(0, 4, text_units, 0)

    def ring_copy(k, src, dst, target):
        return pltpu.make_async_remote_copy(
            src_ref=kv.at[src],
            dst_ref=kv.at[dst],
            send_sem=b_send.at[k],
            recv_sem=b_recv.at[dst],
            device_id={"seq": target},
            device_id_type=MESH,
        )

    copies = {
        0: (ring_copy(0, 0, 4, right), ring_copy(1, 0, 5, left), ring_copy(2, 0, 2, sibling)),
        1: (ring_copy(3, 1, 8, right), ring_copy(4, 1, 9, left), ring_copy(5, 1, 3, sibling)),
        2: (ring_copy(6, 4 + core, 12, far), ring_copy(7, 4, 6, sibling), ring_copy(8, 5, 7, sibling)),
        3: (ring_copy(9, 8 + core, 14, far), ring_copy(10, 8, 10, sibling), ring_copy(11, 9, 11, sibling)),
        4: (ring_copy(12, 12, 13, sibling),),
        5: (ring_copy(13, 14, 15, sibling),),
    }

    def arrived(dst):
        ring_copy(0, dst, dst, sibling).wait_recv()

    def send(stage):
        for copy in copies[stage]:
            copy.start()

    for d in (2, 6, 4):
        kv_copy(d).wait_recv()
    send(0)
    for d in (1, 7, 3, 5):
        kv_copy(d).wait_recv()
    send(1)

    s_bufs = (s0, s1)
    p_bufs = (p0, p1)

    def scores(step, r, h, buf):
        t = r // GROUP_HEADS
        best = None
        for side in range(2):
            slot = 2 * step + side
            if h < 4:
                lhs = jnp.concatenate(
                    [kv[slot, b, 128 * (h // 2) : 128 * (h // 2 + 1), :] for b in range(4)], 0
                )
                s = jnp.dot(lhs, qx[6 * t + h], preferred_element_type=f32)
                buf[512 * side : 512 * (side + 1), :] = s
                top = jnp.max(s.reshape(64, 8, TILE), axis=0)
                best = top if best is None else jnp.maximum(best, top)
            else:
                lhs = jnp.concatenate([kv[slot, b, 256:320, :] for b in range(4)], 0)
                for half in range(2):
                    s = jnp.dot(lhs, qx[6 * t + 4 + half], preferred_element_type=f32)
                    for b in range(4):
                        at = 512 * side + 128 * b + HDIM * half
                        buf[at : at + HDIM, :] = s[HDIM * b : HDIM * (b + 1)]
                    top = jnp.max(s.reshape(32, 8, TILE), axis=0)
                    best = top if best is None else jnp.maximum(best, top)
        old = m_ref[r]
        new = jnp.maximum(old, jnp.max(best, axis=0, keepdims=True))
        m_ref[r] = new
        return new, jnp.exp2((old - new) * SCORE_SCALE)

    def weigh(buf, top, out):
        for j in range(4):
            rows = slice(256 * j, 256 * (j + 1))
            out[rows, :] = jnp.exp2((buf[rows, :] - top) * SCORE_SCALE).astype(bf16)

    def add_values(step, r, h, rescale, buf):
        total = None
        for side in range(2):
            slot = 2 * step + side
            rows = FEATURES + HDIM * h
            lhs = jnp.concatenate([kv[slot, b, rows : rows + HDIM, :] for b in range(4)], 1)
            part = jnp.dot(
                jnp.concatenate([lhs, ones], 0),
                buf[512 * side : 512 * (side + 1), :],
                preferred_element_type=f32,
            )
            total = part if total is None else total + part
        acc[r] = acc[r] * rescale + total

    def one_step(step, _):
        @pl.when(step == 1)
        def _():
            arrived(2)
            arrived(3)

        @pl.when(step == 2)
        def _():
            arrived(4)
            arrived(5)
            send(2)

        @pl.when(step == 3)
        def _():
            arrived(6)
            arrived(7)

        @pl.when(step == 4)
        def _():
            arrived(8)
            arrived(9)
            send(3)

        @pl.when(step == 5)
        def _():
            arrived(10)
            arrived(11)

        @pl.when(step == 6)
        def _():
            arrived(12)
            send(4)
            arrived(13)

        @pl.when(step == 7)
        def _():
            arrived(14)
            send(5)
            arrived(15)

        p1[...] = jnp.zeros_like(p1)
        top, rescale = scores(step, 0, 0, s0)

        def ten(i, carry):
            top, rescale, before = carry
            for j in range(10):
                r = 10 * i + j
                last_r = jnp.maximum(r - 1, 0)
                next_r = lax.rem(r + 1, 20)
                add_values(step, last_r, (j - 1) % 5, before, p_bufs[(j + 1) % 2])
                weigh(s_bufs[j % 2], top, p_bufs[j % 2])
                if j < 9:
                    following = scores(step, r + 1, (j + 1) % 5, s_bufs[(j + 1) % 2])
                else:
                    following = scores(step, next_r, 0, s_bufs[0])
                before = rescale
                top, rescale = following
            return top, rescale, before

        top, rescale, before = lax.fori_loop(0, 2, ten, (top, rescale, jnp.ones_like(top)))
        add_values(step, 19, 4, before, p1)
        return 0

    lax.fori_loop(0, 8, one_step, 0)

    def finish(t, _):
        for h in range(GROUP_HEADS):
            sums = acc[GROUP_HEADS * t + h]
            gain = mask_ref[GROUP_HEADS * group + h].astype(f32)
            out = (sums[:HDIM] / sums[HDIM : HDIM + 1] * gain).astype(bf16)
            o_stage[2 * t, HDIM * h : HDIM * (h + 1), :] = out[:, :128]
            o_stage[2 * t + 1, HDIM * h : HDIM * (h + 1), :] = out[:, 128:]
        return 0

    lax.fori_loop(0, 4, finish, 0)

    def o_copy(d):
        peer = lax.rem(group + d, 8)
        return pltpu.make_async_remote_copy(
            src_ref=o_stage.at[peer],
            dst_ref=o_ref.at[group],
            send_sem=o_send.at[d],
            recv_sem=o_recv.at[d],
            device_id={"head": peer},
            device_id_type=MESH,
        )

    for d in order:
        o_copy(d).start()
    o_ref[pl.ds(group, 1)] = o_stage[pl.ds(group, 1)]
    for d in order:
        q_copy(d).wait_send()
        kv_copy(d).wait_send()
    for stage in copies.values():
        for copy in stage:
            copy.wait_send()
    for d in order:
        o_copy(d).wait_recv()
        o_copy(d).wait_send()


def attend(q, k, v, text_k, text_v, bias, head_mask):
    vmem = functools.partial(pltpu.VMEM)
    dma = pltpu.SemaphoreType.DMA
    anywhere = pl.BlockSpec(memory_space=pl.ANY)
    return pl.pallas_call(
        attention_kernel,
        out_shape=jax.ShapeDtypeStruct((8, FEATURES, TOKENS), bf16),
        in_specs=[anywhere] * 5
        + [pl.BlockSpec(memory_space=pltpu.VMEM), pl.BlockSpec(memory_space=pltpu.SMEM)],
        out_specs=pl.BlockSpec(memory_space=pltpu.VMEM),
        scratch_shapes=[
            vmem((3, TOKENS, 2560), bf16),
            vmem((2, SLOTS, 384), bf16),
            vmem((8, FEATURES, TOKENS), bf16),
            vmem((8, 2 * FEATURES, TOKENS), bf16),
            vmem((8, FEATURES, TOKENS), bf16),
            vmem((8, FEATURES, TOKENS), bf16),
            vmem((16, 4, 2 * FEATURES, TOKENS), bf16),
            vmem((24, 128, TILE), bf16),
            vmem((3, SLOTS, 128), bf16),
            vmem((384, SLOTS), bf16),
            vmem((QUERIES, TILE), f32),
            vmem((QUERIES, TILE), f32),
            vmem((QUERIES, TILE), bf16),
            vmem((QUERIES, TILE), bf16),
            vmem((20, 1, TILE), f32),
            vmem((20, 80, TILE), f32),
            dma((5,)),
            dma((8,)),
            dma((8,)),
            dma((8,)),
            dma((8,)),
            dma((14,)),
            dma((16,)),
            dma((8,)),
            dma((8,)),
        ],
        compiler_params=pltpu.CompilerParams(
            collective_id=0, has_side_effects=True, vmem_limit_bytes=48 << 20
        ),
        cost_estimate=pl.CostEstimate(
            flops=40_000_000_000, bytes_accessed=8_000_000, transcendentals=44_000_000
        ),
    )(q, k, v, text_k, text_v, bias, head_mask)


def gather_weight(out_weight):
    core = lax.axis_index("seq") % 2
    rows = out_weight.shape[0] // 2
    mine = lax.dynamic_slice_in_dim(out_weight, core * rows, rows, 0)
    mine = lax.all_gather(mine, "head", axis=0, tiled=False)
    other = lax.ppermute(mine, "seq", [(i, i ^ 1) for i in range(8)])
    first = jnp.where(core == 0, mine, other)
    second = jnp.where(core == 0, other, mine)
    return jnp.stack([first, second], 1).reshape(-1, out_weight.shape[1])


def shards(
    q_img,
    k_img,
    v_img,
    text_k,
    text_v,
    text_len,
    head_mask,
    hidden,
    out_weight,
    out_bias,
    final_shift,
    final_scale,
    final_weight,
    latent,
    step_index,
):
    live = jnp.arange(SLOTS) < text_len[0]
    bias = jnp.broadcast_to(jnp.where(live, 0.0, -1e30).astype(f32)[:, None], (SLOTS, TILE))
    attended = attend(q_img, k_img, v_img, text_k, text_v, bias, head_mask)
    attended = attended.reshape(8 * FEATURES, TOKENS)
    own_rows = hidden.shape[1]
    projected = lax.dot_general(
        attended,
        lax.all_gather(out_weight, "head", axis=0, tiled=True),
        (((0,), (0,)), ((), ())),
        preferred_element_type=jnp.float32,
    )
    residual = hidden[0].astype(jnp.float32) + projected + out_bias.astype(jnp.float32)
    centre = jnp.mean(residual, axis=1, keepdims=True)
    spread = jnp.mean((residual - centre) ** 2, axis=1, keepdims=True)
    normed = (residual - centre) / jnp.sqrt(spread + 1e-06)
    modulated = (
        normed * (1.0 + final_scale[0].astype(jnp.float32)) + final_shift[0].astype(jnp.float32)
    ).astype(jnp.bfloat16)
    velocity = jnp.einsum("cd,td->ct", final_weight, modulated, preferred_element_type=jnp.float32)
    channel_half = velocity.shape[0] // 2
    halves = velocity.reshape(2, 1, channel_half, own_rows)
    branches = lax.all_to_all(
        halves.astype(jnp.bfloat16), "cfg", split_axis=0, concat_axis=1, tiled=True
    ).astype(halves.dtype)
    cond_velocity = branches[0, 0]
    uncond_velocity = branches[0, 1]
    guided = uncond_velocity + GUIDANCE * (cond_velocity - uncond_velocity)
    sigma_now = sigma_at(step_index[0])
    sigma_next = sigma_at(step_index[0] + 1)
    denoised = latent - sigma_now * guided
    next_latent = latent + (sigma_next - sigma_now) * guided
    return (next_latent, denoised)


def solution(mesh):
    in_specs = (
        P("cfg", ("seq", "head"), None),
        P("cfg", ("seq", "head"), None),
        P("cfg", ("seq", "head"), None),
        P("cfg", None, None),
        P("cfg", None, None),
        P("cfg"),
        P(),
        P("cfg", ("seq", "head"), None),
        P("head", None),
        P(),
        P("cfg", None),
        P("cfg", None),
        P(),
        P("cfg", ("seq", "head")),
        P(),
    )
    out_specs = (P("cfg", ("seq", "head")), P("cfg", ("seq", "head")))
    return jax.shard_map(shards, mesh=mesh, in_specs=in_specs, out_specs=out_specs, check_vma=False)
```

profile of v0, /device:TPU:1, one launch (start us, length us, event | category | flops | bytes accessed | tf_op | source)
XLA Modules:
  0.0 202.6 jit_solution(4182000252557653222)
XLA Ops:
  7.2 0.0 copy-start
  7.2 0.0 copy-start.9
  7.2 0.0 copy-start.7
  7.2 0.0 copy-start.8
  7.2 0.0 copy-start.1
  7.2 0.0 copy-start.5
  7.2 0.0 all-gather.2.cloned.1.call-start
  7.3 0.7 all-gather.2.cloned.1.call-update
  8.6 0.0 copy-done.9
  8.6 0.0 copy-done.7
  8.7 0.0 copy-done.8
  8.7 0.1 convert_reduce_fusion
  8.7 0.1 broadcast_in_dim.12.bias_ref
  8.8 0.0 copy-done.1
  8.9 0.0 copy-done.5
  8.9 0.0 copy-start.2
  8.9 1.1 copy-done.2
  10.0 0.0 copy-start.3
  10.0 1.1 copy-done.3
  11.0 0.0 copy-start.4
  11.0 1.1 copy-done.4
  12.1 118.8 %shard_map.158 = bf16[8,320,128]{2,1,0:T(8,128)(2,1)S(1)} custom-call(bf16[1,128,2560]{2,1,0:T(8,128)(2,1)S(1)} %copy-done.2, bf16[1,128,2560]{2,1,0:T(8,128)(2,1)S(1)} %copy-done.3, bf16[1,128,2560]{2,1,0:T(8,128)(2,1)S(1)} %copy-done.4, bf16[1,384,2560]{2,1,0:T(8,128)(2,1)S(1)} %copy-done.1, bf16[1,384,2560]{2,1,0:T(8,128)(2,1)} %tv_hbm.1, ...), custom_call_target="tpu_custom_call" | custom-call | flops 40000000000 | bytes 8000000 | tf_op jit(solution)/shard_map/pallas_call | solution.py:399
  130.9 50.3 %all-gather.2.cloned.1.call-done = bf16[2560,2432]{1,0:T(8,128)(2,1)} async-done(((bf16[320,2432]{1,0:T(8,128)(2,1)}), bf16[2560,2432]{1,0:T(8,128)(2,1)}) %all-gather.2.cloned.1.call-update) | async-done | bytes 12451856 | tf_op jit(solution)/shard_map/all_gather | solution.py:476
  181.2 6.6 %fusion.5 = (f32[128]{0:T(128)S(1)}, f32[128,2432]{1,0:T(8,128)S(1)}) fusion(f32[2432]{0:T(1024)S(1)} %convert_element_type.61, bf16[2560,128]{1,0:T(8,128)(2,1)S(1)} %bitcast.39, bf16[2560,2432]{1,0:T(8,128)(2,1)} %all-gather.2.cloned.1.call-done, bf16[1,128,2432]{2,1,0:T(8,128)(2,1)} %param.22), kind=kOutput, calls=%fused_computation.19 | convolution fusion | flops 1595080576 | bytes 14985216 | tf_op jit(solution)/shard_map/dot_general | solution.py:474
  187.9 0.3 multiply_reduce_fusion
  188.2 0.0 copy-done
  188.2 0.0 copy-start.6
  188.2 1.1 convolution_convert_fusion
  189.2 3.2 %all-to-all-start = ((bf16[2,1,32,128]{3,2,1,0:T(8,128)(2,1)}), bf16[2,1,32,128]{3,2,1,0:T(8,128)(2,1)S(1)}, u32[]{:S(2)}, u32[]{:S(2)}) async-start(bf16[2,1,32,128]{3,2,1,0:T(8,128)(2,1)} %bitcast.7), calls=%async_computation | async-start | bytes 32768 | tf_op jit(solution)/shard_map/all_to_all | solution.py:490
  193.2 2.0 all-to-all-done
  195.2 0.0 copy-done.6
  195.2 0.6 multiply_subtract_fusion
  (5 shorter events, 0.0 us)
Async XLA Ops:
  7.2 181.0 %copy-start = (bf16[64,2432]{1,0:T(8,128)(2,1)S(1)}, bf16[64,2432]{1,0:T(8,128)(2,1)}, u32[]{:S(2)}) copy-start(bf16[64,2432]{1,0:T(8,128)(2,1)} %param.27) | copy-start | bytes 933892
  7.2 1.4 copy-start.9
  7.2 1.5 copy-start.7
  7.2 1.5 copy-start.8
  7.2 1.6 copy-start.1
  7.2 1.6 copy-start.5
  7.2 174.0 %all-gather.2.cloned.1.call-start = ((), (), s32[]{:S(2)}) async-start(), calls=%async_computation.1 | async-start | bytes 14008320 | tf_op jit(solution)/shard_map/all_gather | solution.py:476
  8.9 1.1 copy-start.2
  10.0 1.1 copy-start.3
  11.0 1.1 copy-start.4
  188.2 7.0 %copy-start.6 = (f32[32,128]{1,0:T(8,128)S(1)}, f32[32,128]{1,0:T(8,128)}, u32[]{:S(2)}) copy-start(f32[32,128]{1,0:T(8,128)} %param.28) | copy-start | bytes 49156
  189.2 5.9 %all-to-all-start = ((bf16[2,1,32,128]{3,2,1,0:T(8,128)(2,1)}), bf16[2,1,32,128]{3,2,1,0:T(8,128)(2,1)S(1)}, u32[]{:S(2)}, u32[]{:S(2)}) async-start(bf16[2,1,32,128]{3,2,1,0:T(8,128)(2,1)} %bitcast.7), calls=%async_computation | async-start | bytes 32768 | tf_op jit(solution)/shard_map/all_to_all | solution.py:490
Sparse Core Ops, SparseCore 0:
  10.4 170.7 all-gather.1
where the time goes:
time: 204 us; the launch traced here: 203 us
  Pallas kernels  119 us (58%)
  waiting for transfers between devices  52.9 us (26%)
  between operations  15.6 us (8%)
  matrix products  7.68 us (4%)
  local copies, waits for them, and re-layouts  3.4 us (2%)
  starting transfers between devices  3.27 us (2%)
    pallas_call x1, Pallas kernels, attend(): pl.pallas_call(attention_kernel, out_shape=jax.ShapeDtypeStruct((8, FEATU...  119 us
    all_gather x1, waiting for transfers between devices, shards(): lax.all_gather(out_weight, 'head', axis=0, tiled=True)  50.3 us
    dot_general x1, matrix products, shards(): lax.dot_general(attended, lax.all_gather(out_weight, 'head', axis=0, tile...  6.63 us
  transfers between devices with their start and end apart: 2, of which 2 were waited for; matrix products, arithmetic and copies ran while one was open for 0% of the time, Pallas kernels for 59%

commit v1 on v0

v1 whole, which is shorter than its diff:
```python
import functools

import jax
import jax.numpy as jnp
from jax import lax
from jax.experimental import pallas as pl
from jax.experimental.pallas import tpu as pltpu
from jax.sharding import PartitionSpec as P

HDIM = 64
STEPS = 28
GUIDANCE = 3.5
GROUP_HEADS = 5
FEATURES = 320
TOKENS = 128
SLOTS = 384
QUERIES = 1024
TILE = 256
SCORE_SCALE = 0.125 * 1.4426950408889634
MESH = pl.DeviceIdType.MESH
f32 = jnp.float32
bf16 = jnp.bfloat16


def sigma_at(position):
    level = 1.0 - position.astype(jnp.float32) / STEPS
    return 3.0 * level / (1.0 + 2.0 * level)


def block_kernel(
    q_hbm,
    k_hbm,
    v_hbm,
    tk_hbm,
    tv_hbm,
    w_hbm,
    hidden_hbm,
    len_ref,
    mask_ref,
    step_ref,
    out_bias,
    shift_ref,
    scale_ref,
    final_weight,
    latent_ref,
    next_ref,
    denoised_ref,
    loaded,
    text_slab,
    q_stage,
    kv_stage,
    o_stage,
    q_recv,
    o_recv,
    kv,
    weight,
    qx,
    text_keys,
    text_values,
    s0,
    s1,
    p0,
    p1,
    m_ref,
    acc,
    hidden,
    attended,
    residual,
    v_stage,
    v_recv,
    load_sem,
    q_send,
    q_recv_sem,
    a_send,
    a_recv,
    b_send,
    b_recv,
    o_send,
    o_recv_sem,
    w_send,
    w_recv,
    v_sem,
):
    cfg = lax.axis_index("cfg")
    seq = lax.axis_index("seq")
    group = lax.axis_index("head")
    core = lax.rem(seq, 2)
    parity = lax.rem(group, 2)
    row = group // 2
    right = lax.rem(seq + 2, 8)
    left = lax.rem(seq + 6, 8)
    sibling = seq + 1 - 2 * core
    far = lax.rem(seq + 2 + 4 * core, 8)
    turned = group + 1 - 2 * parity
    w_right = lax.rem(group + 2, 8)
    w_left = lax.rem(group + 6, 8)
    w_opposite = lax.rem(group + 4, 8)
    w_far = lax.rem(group + 2 + 4 * core, 8)

    slab_start = pl.multiple_of(128 * ((5 * group) // 2), 128)
    loads = (
        [
            pltpu.make_async_copy(src.at[0], loaded.at[i], load_sem.at[i])
            for i, src in enumerate((q_hbm, k_hbm, v_hbm))
        ]
        + [
            pltpu.make_async_copy(
                src.at[0, :, pl.ds(slab_start, 384)], text_slab.at[i], load_sem.at[3 + i]
            )
            for i, src in enumerate((tk_hbm, tv_hbm))
        ]
        + [
            pltpu.make_async_copy(
                w_hbm.at[pl.ds(160 * i, 160)], weight.at[2 * group + i], load_sem.at[5 + i]
            )
            for i in range(2)
        ]
        + [pltpu.make_async_copy(hidden_hbm.at[0], hidden, load_sem.at[7])]
    )
    for load in loads:
        load.start()

    barrier = pltpu.get_barrier_semaphore()
    for d in range(1, 8):
        pl.semaphore_signal(
            barrier, inc=1, device_id={"head": lax.rem(group + d, 8)}, device_id_type=MESH
        )
    for near in (right, left, sibling):
        pl.semaphore_signal(barrier, inc=1, device_id={"seq": near}, device_id_type=MESH)
    pl.semaphore_signal(barrier, inc=1, device_id={"cfg": 1 - cfg}, device_id_type=MESH)
    pl.semaphore_signal(
        barrier, inc=1, device_id={"cfg": 1 - cfg, "head": turned}, device_id_type=MESH
    )

    low = lax.broadcasted_iota(jnp.int32, (TOKENS, 128), 1) < HDIM
    low_half = lax.broadcasted_iota(jnp.int32, (HDIM, 128), 1) < HDIM

    loads[0].wait()
    for i in range(20):
        block = loaded[0, :, 128 * i : 128 * (i + 1)].T
        for half in range(2):
            f = 128 * i + HDIM * half
            q_stage[f // FEATURES, pl.ds(f % FEATURES, HDIM), :] = block[
                HDIM * half : HDIM * (half + 1)
            ]
    pl.semaphore_wait(barrier, 12)

    def head_copy(src, dst, send, recv, d):
        peer = lax.rem(group + d, 8)
        return pltpu.make_async_remote_copy(
            src_ref=src.at[peer],
            dst_ref=dst.at[d % 2, row],
            send_sem=send.at[d],
            recv_sem=recv.at[d],
            device_id={"head": peer},
            device_id_type=MESH,
        )

    def q_copy(d):
        return head_copy(q_stage, q_recv, q_send, q_recv_sem, d)

    def kv_copy(d):
        return head_copy(kv_stage, kv, a_send, a_recv, d)

    along = (2, 6, 4)
    across = (1, 7, 3, 5)
    for d in along:
        q_copy(d).start()
    q_recv[0, pl.ds(row, 1)] = q_stage[pl.ds(group, 1)]

    loads[1].wait()
    loads[2].wait()
    for p in range(8):
        first = (5 * p) // 2
        tiles = [
            loaded[1, :, 128 * (first + i) : 128 * (first + i + 1)].astype(f32) for i in range(3)
        ]
        if p % 2 == 0:
            kv_stage[p, 0:128, :] = tiles[0].astype(bf16)
            kv_stage[p, 128:256, :] = tiles[1].astype(bf16)
            last = jnp.where(low_half, tiles[2][:HDIM], pltpu.roll(tiles[2][HDIM:], HDIM, 1))
        else:
            kv_stage[p, 0:128, :] = jnp.where(low, tiles[1], tiles[0]).astype(bf16)
            kv_stage[p, 128:256, :] = jnp.where(low, tiles[2], tiles[1]).astype(bf16)
            last = jnp.where(low_half, pltpu.roll(tiles[2][:HDIM], HDIM, 1), tiles[2][HDIM:])
        kv_stage[p, 256:320, :] = last.astype(bf16)
    for i in range(20):
        block = loaded[2, :, 128 * i : 128 * (i + 1)].T
        for half in range(2):
            f = 128 * i + HDIM * half
            kv_stage[f // FEATURES, pl.ds(FEATURES + f % FEATURES, HDIM), :] = block[
                HDIM * half : HDIM * (half + 1)
            ]
    for d in along:
        kv_copy(d).start()
    for d in across:
        q_copy(d).start()
    for d in across:
        kv_copy(d).start()
    kv[0, pl.ds(row, 1)] = kv_stage[pl.ds(group, 1)]

    loads[3].wait()
    loads[4].wait()
    odd = parity == 1
    swap = jnp.logical_and(lax.broadcasted_iota(jnp.int32, (SLOTS, 128), 1) < HDIM, odd)
    slabs = [text_slab[0, :, 128 * i : 128 * (i + 1)].astype(f32) for i in range(3)]
    text_keys[0] = jnp.where(swap, slabs[1], slabs[0]).astype(bf16)
    text_keys[1] = jnp.where(swap, slabs[2], slabs[1]).astype(bf16)
    text_keys[2] = slabs[2].astype(bf16)
    for i in range(3):
        for j in range(3):
            text_values[128 * i : 128 * (i + 1), 128 * j : 128 * (j + 1)] = text_slab[
                1, 128 * j : 128 * (j + 1), 128 * i : 128 * (i + 1)
            ].T

    zero = jnp.zeros((HDIM, TILE), bf16)
    ones = jnp.ones((16, 512), bf16)

    def queries_and_text(t, _):
        dead = lax.broadcasted_iota(jnp.int32, (SLOTS, TILE), 0) >= len_ref[0]
        for h in range(GROUP_HEADS):
            rows = slice(HDIM * h, HDIM * (h + 1))
            q = jnp.concatenate(
                [q_recv[t // 2, 2 * (t % 2), rows], q_recv[t // 2, 2 * (t % 2) + 1, rows]], 1
            )
            if h < 4:
                offset = parity if h % 2 == 0 else 1 - parity
                qx[6 * t + h, pl.ds(pl.multiple_of(HDIM * offset, HDIM), HDIM), :] = q
                qx[6 * t + h, pl.ds(pl.multiple_of(HDIM * (1 - offset), HDIM), HDIM), :] = zero
            else:
                for side in range(2):
                    qx[6 * t + 4 + side, HDIM * side : HDIM * (side + 1), :] = q
                    qx[6 * t + 4 + side, HDIM * (1 - side) : HDIM * (2 - side), :] = zero
        for h in range(GROUP_HEADS):
            weights_at = 6 * t + h if h < 4 else 6 * t + 4 + parity
            s = jnp.dot(text_keys[h // 2], qx[weights_at], preferred_element_type=f32)
            s = jnp.where(dead, -1e30, s)
            top = jnp.max(s, axis=0, keepdims=True)
            p = jnp.exp2((s - top) * SCORE_SCALE).astype(bf16)
            values = text_values[pl.ds(pl.multiple_of(HDIM * (parity + h), HDIM), HDIM), :]
            acc[GROUP_HEADS * t + h] = jnp.dot(
                jnp.concatenate([values, ones[:, :SLOTS]], 0), p, preferred_element_type=f32
            )
            m_ref[GROUP_HEADS * t + h] = top
        return 0

    for d in along:
        q_copy(d).wait_recv()
    lax.fori_loop(0, 2, queries_and_text, 0)

    def ring_copy(k, src, dst, target):
        return pltpu.make_async_remote_copy(
            src_ref=kv.at[src],
            dst_ref=kv.at[dst],
            send_sem=b_send.at[k],
            recv_sem=b_recv.at[dst],
            device_id={"seq": target},
            device_id_type=MESH,
        )

    copies = {
        0: (ring_copy(2, 0, 2, sibling), ring_copy(0, 0, 4, right), ring_copy(1, 0, 5, left)),
        1: (ring_copy(5, 1, 3, sibling), ring_copy(3, 1, 8, right), ring_copy(4, 1, 9, left)),
        2: (ring_copy(6, 4 + core, 12, far), ring_copy(7, 4, 6, sibling), ring_copy(8, 5, 7, sibling)),
        3: (ring_copy(9, 8 + core, 14, far), ring_copy(10, 8, 10, sibling), ring_copy(11, 9, 11, sibling)),
        4: (ring_copy(12, 12, 13, sibling),),
        5: (ring_copy(13, 14, 15, sibling),),
    }

    def arrived(*slots):
        for dst in slots:
            ring_copy(0, dst, dst, sibling).wait_recv()

    def send(stage):
        for copy in copies[stage]:
            copy.start()

    def weight_copy(k, owner, target, from_hbm=False):
        at = 2 * owner + core
        return pltpu.make_async_remote_copy(
            src_ref=w_hbm.at[pl.ds(pl.multiple_of(160 * core, 160), 160)] if from_hbm else weight.at[at],
            dst_ref=weight.at[at],
            send_sem=w_send.at[k],
            recv_sem=w_recv.at[k],
            device_id=target,
            device_id_type=MESH,
        )

    to_right, to_left = {"head": w_right}, {"head": w_left}
    to_turned = {"cfg": 1 - cfg, "head": turned}
    to_sibling = {"seq": sibling}
    owners = (
        w_left,
        w_right,
        turned,
        w_opposite,
        lax.rem(turned + 6, 8),
        lax.rem(turned + 2, 8),
        lax.rem(turned + 4, 8),
    )
    weight_copies = {
        0: (
            weight_copy(0, group, to_right, True),
            weight_copy(1, group, to_left, True),
            weight_copy(2, group, to_turned, True),
        ),
        1: (
            weight_copy(3, lax.rem(group + 6 + 4 * core, 8), {"head": w_far}),
            weight_copy(4, turned, to_right),
            weight_copy(5, turned, to_left),
        ),
        2: (weight_copy(6, w_opposite, to_turned),),
    }
    to_core = [weight_copy(7 + k, owners[k], to_sibling) for k in range(7)]

    def weight_arrived(*which):
        for k in which:
            weight_copy(k, group, to_sibling).wait_recv()

    def weight_send(stage):
        for copy in weight_copies[stage]:
            copy.start()

    def share(*which):
        for k in which:
            to_core[k].start()

    s_bufs = (s0, s1)
    p_bufs = (p0, p1)

    def scores(step, r, t, h, buf):
        best = None
        for side in range(2):
            slot = step[side]
            if h < 4:
                lhs = jnp.concatenate(
                    [kv[slot, b, 128 * (h // 2) : 128 * (h // 2 + 1), :] for b in range(4)], 0
                )
                s = jnp.dot(lhs, qx[6 * t + h], preferred_element_type=f32)
                buf[512 * side : 512 * (side + 1), :] = s
                top = jnp.max(s.reshape(64, 8, TILE), axis=0)
                best = top if best is None else jnp.maximum(best, top)
            else:
                lhs = jnp.concatenate([kv[slot, b, 256:320, :] for b in range(4)], 0)
                for half in range(2):
                    s = jnp.dot(lhs, qx[6 * t + 4 + half], preferred_element_type=f32)
                    for b in range(4):
                        at = 512 * side + 128 * b + HDIM * half
                        buf[at : at + HDIM, :] = s[HDIM * b : HDIM * (b + 1)]
                    top = jnp.max(s.reshape(32, 8, TILE), axis=0)
                    best = top if best is None else jnp.maximum(best, top)
        old = m_ref[r]
        new = jnp.maximum(old, jnp.max(best, axis=0, keepdims=True))
        m_ref[r] = new
        return new, jnp.exp2((old - new) * SCORE_SCALE)

    def weigh(buf, top, out):
        for j in range(4):
            rows = slice(256 * j, 256 * (j + 1))
            out[rows, :] = jnp.exp2((buf[rows, :] - top) * SCORE_SCALE).astype(bf16)

    def add_values(step, r, h, rescale, buf):
        total = None
        for side in range(2):
            slot = step[side]
            rows = FEATURES + HDIM * h
            lhs = jnp.concatenate([kv[slot, b, rows : rows + HDIM, :] for b in range(4)], 1)
            part = jnp.dot(
                jnp.concatenate([lhs, ones], 0),
                buf[512 * side : 512 * (side + 1), :],
                preferred_element_type=f32,
            )
            total = part if total is None else total + part
        acc[r] = acc[r] * rescale + total

    def finish(t, _):
        for h in range(GROUP_HEADS):
            sums = acc[GROUP_HEADS * t + h]
            gain = mask_ref[GROUP_HEADS * group + h].astype(f32)
            out = (sums[:HDIM] / sums[HDIM : HDIM + 1] * gain).astype(bf16)
            for side in range(2):
                o_stage[t // 2, 2 * (t % 2) + side, HDIM * h : HDIM * (h + 1), :] = out[
                    :, 128 * side : 128 * (side + 1)
                ]
        return 0

    def o_copy(d):
        peer = lax.rem(group + d, 8)
        return pltpu.make_async_remote_copy(
            src_ref=o_stage.at[d % 2, peer // 2],
            dst_ref=o_recv.at[group],
            send_sem=o_send.at[d],
            recv_sem=o_recv_sem.at[d],
            device_id={"head": peer},
            device_id_type=MESH,
        )

    def at_start(half):
        @pl.when(half == 0)
        def _():
            for d in along:
                kv_copy(d).wait_recv()
            send(0)
            arrived(2)

        @pl.when(half == 1)
        def _():
            for d in across:
                q_copy(d).wait_recv()
            lax.fori_loop(2, 4, queries_and_text, 0)

        @pl.when(half == 2)
        def _():
            for d in across:
                kv_copy(d).wait_recv()
            send(1)
            weight_send(0)
            arrived(3)

        @pl.when(half == 4)
        def _():
            arrived(4, 5)
            send(2)

        @pl.when(half == 6)
        def _():
            arrived(6, 7)

        @pl.when(half == 7)
        def _():
            arrived(12)
            send(4)

        @pl.when(half == 8)
        def _():
            arrived(13)
            weight_arrived(0, 1, 2)
            weight_send(1)
            share(0, 1, 2)

        @pl.when(half == 10)
        def _():
            arrived(8, 9)
            send(3)

        @pl.when(half == 11)
        def _():
            weight_arrived(3)
            weight_send(2)
            share(3)

        @pl.when(half == 12)
        def _():
            arrived(10, 11)

        @pl.when(half == 13)
        def _():
            arrived(14)
            send(5)

        @pl.when(half == 14)
        def _():
            arrived(15)

        @pl.when(half == 15)
        def _():
            lax.fori_loop(2, 4, finish, 0)
            for d in across:
                o_copy(d).start()

    def half_step(half, _):
        at_start(half)
        order = half // 2
        slots = (
            jnp.where(order == 0, 0, jnp.where(order == 1, 1, 0)),
            jnp.where(order == 0, 2, jnp.where(order == 1, 3, 0)),
        )
        pair = jnp.where(
            order < 4, order, jnp.where(order == 4, 6, jnp.where(order < 7, order - 1, 7))
        )
        one = jnp.where(order < 2, slots[0], 2 * pair)
        two = jnp.where(order < 2, slots[1], 2 * pair + 1)
        side = jnp.where(order == 7, 1 - half % 2, half % 2)
        where = (one, two)

        def unit(j):
            return 10 * side + j, 2 * side + j // 5, j % 5

        top, rescale = scores(where, *unit(0), s0)
        before = None
        for j in range(10):
            if j > 0:
                r, t, h = unit(j - 1)
                add_values(where, r, h, before, p_bufs[(j + 1) % 2])
            weigh(s_bufs[j % 2], top, p_bufs[j % 2])
            before = rescale
            if j < 9:
                top, rescale = scores(where, *unit(j + 1), s_bufs[(j + 1) % 2])
        r, t, h = unit(9)
        add_values(where, r, h, before, p1)
        return 0

    lax.fori_loop(0, 16, half_step, 0)

    lax.fori_loop(0, 2, finish, 0)
    for d in along:
        o_copy(d).start()
    weight_arrived(4, 5, 6)
    share(4, 5, 6)
    o_recv[pl.ds(group, 1)] = o_stage[0, pl.ds(row, 1)]

    for d in along + across:
        q_copy(d).wait_send()
        kv_copy(d).wait_send()
    for stage in copies.values():
        for copy in stage:
            copy.wait_send()
    for stage in weight_copies.values():
        for copy in stage:
            copy.wait_send()

    for d in across + along:
        o_copy(d).wait_recv()
    for p in range(8):
        for h in range(GROUP_HEADS):
            f = FEATURES * p + HDIM * h
            if f % 128 == 0:
                q = f // 128
                lo = o_recv[p, HDIM * h : HDIM * (h + 1), :]
                nxt = f + HDIM
                hi = o_recv[nxt // FEATURES, nxt % FEATURES : nxt % FEATURES + HDIM, :]
                attended[:, 128 * q : 128 * (q + 1)] = jnp.concatenate([lo, hi], 0).T
    for load in loads[5:]:
        load.wait()
    weight_arrived(7, 8, 9, 10, 11, 12, 13)
    rows = attended[...]
    width = 2432
    total = None
    for n in range(0, width, TILE):
        cols = slice(n, min(n + TILE, width))
        part = jnp.dot(
            rows,
            jnp.concatenate([weight[i, :, cols] for i in range(16)], 0),
            preferred_element_type=f32,
        )
        part = hidden[:, cols].astype(f32) + part + out_bias[:, cols].astype(f32)
        residual[:, cols] = part
        part = jnp.sum(part, axis=1, keepdims=True)
        total = part if total is None else total + part
    centre = total / width
    total = None
    for n in range(0, width, TILE):
        cols = slice(n, min(n + TILE, width))
        part = residual[:, cols] - centre
        residual[:, cols] = part
        part = jnp.sum(part * part, axis=1, keepdims=True)
        total = part if total is None else total + part
    norm = 1.0 / jnp.sqrt(total / width + 1e-06)
    velocity = None
    for n in range(0, width, TILE):
        cols = slice(n, min(n + TILE, width))
        modulated = residual[:, cols] * norm * (1.0 + scale_ref[:, cols].astype(f32)) + shift_ref[
            :, cols
        ].astype(f32)
        part = lax.dot_general(
            final_weight[:, cols],
            modulated.astype(bf16),
            (((1,), (1,)), ((), ())),
            preferred_element_type=f32,
        )
        velocity = part if velocity is None else velocity + part
    v_stage[0] = velocity[:32].astype(bf16)
    v_stage[1] = velocity[32:].astype(bf16)
    exchange = pltpu.make_async_remote_copy(
        src_ref=v_stage.at[1 - cfg],
        dst_ref=v_recv,
        send_sem=v_sem.at[0],
        recv_sem=v_sem.at[1],
        device_id={"cfg": 1 - cfg},
        device_id_type=MESH,
    )
    exchange.start()
    mine = jnp.where(cfg == 0, velocity[:32], velocity[32:])
    position = jnp.full((32, TOKENS), step_ref[0], jnp.int32)
    sigma_now = sigma_at(position)
    sigma_next = sigma_at(position + 1)
    for d in along + across:
        o_copy(d).wait_send()
    for copy in to_core:
        copy.wait_send()
    exchange.wait()
    theirs = v_recv[...].astype(f32)
    cond = jnp.where(cfg == 0, mine, theirs)
    uncond = jnp.where(cfg == 0, theirs, mine)
    guided = uncond + GUIDANCE * (cond - uncond)
    denoised_ref[...] = latent_ref[...] - sigma_now * guided
    next_ref[...] = latent_ref[...] + (sigma_next - sigma_now) * guided


def shards(
    q_img,
    k_img,
    v_img,
    text_k,
    text_v,
    text_len,
    head_mask,
    hidden,
    out_weight,
    out_bias,
    final_shift,
    final_scale,
    final_weight,
    latent,
    step_index,
):
    vmem = pltpu.VMEM
    dma = pltpu.SemaphoreType.DMA
    anywhere = pl.BlockSpec(memory_space=pl.ANY)
    scalars = pl.BlockSpec(memory_space=pltpu.SMEM)
    whole = pl.BlockSpec(memory_space=pltpu.VMEM)
    out = jax.ShapeDtypeStruct(latent.shape, f32)
    return pl.pallas_call(
        block_kernel,
        out_shape=(out, out),
        in_specs=[anywhere] * 7 + [scalars] * 3 + [whole] * 5,
        out_specs=(whole, whole),
        scratch_shapes=[
            vmem((3, TOKENS, 2560), bf16),
            vmem((2, SLOTS, 384), bf16),
            vmem((8, FEATURES, TOKENS), bf16),
            vmem((8, 2 * FEATURES, TOKENS), bf16),
            vmem((2, 4, FEATURES, TOKENS), bf16),
            vmem((2, 4, FEATURES, TOKENS), bf16),
            vmem((8, FEATURES, TOKENS), bf16),
            vmem((16, 4, 2 * FEATURES, TOKENS), bf16),
            vmem((16, 160, 2432), bf16),
            vmem((24, 128, TILE), bf16),
            vmem((3, SLOTS, 128), bf16),
            vmem((384, SLOTS), bf16),
            vmem((QUERIES, TILE), f32),
            vmem((QUERIES, TILE), f32),
            vmem((QUERIES, TILE), bf16),
            vmem((QUERIES, TILE), bf16),
            vmem((20, 1, TILE), f32),
            vmem((20, 80, TILE), f32),
            vmem((TOKENS, 2432), bf16),
            vmem((TOKENS, 2560), bf16),
            vmem((TOKENS, 2432), f32),
            vmem((2, 32, TOKENS), bf16),
            vmem((32, TOKENS), bf16),
            dma((8,)),
            dma((8,)),
            dma((8,)),
            dma((8,)),
            dma((8,)),
            dma((14,)),
            dma((16,)),
            dma((8,)),
            dma((8,)),
            dma((14,)),
            dma((14,)),
            dma((2,)),
        ],
        compiler_params=pltpu.CompilerParams(
            collective_id=0, has_side_effects=True, vmem_limit_bytes=60 << 20
        ),
        cost_estimate=pl.CostEstimate(
            flops=40_000_000_000, bytes_accessed=20_000_000, transcendentals=44_000_000
        ),
    )(
        q_img,
        k_img,
        v_img,
        text_k,
        text_v,
        out_weight,
        hidden,
        text_len,
        head_mask,
        step_index,
        out_bias[None],
        final_shift,
        final_scale,
        final_weight,
        latent,
    )


def solution(mesh):
    in_specs = (
        P("cfg", ("seq", "head"), None),
        P("cfg", ("seq", "head"), None),
        P("cfg", ("seq", "head"), None),
        P("cfg", None, None),
        P("cfg", None, None),
        P("cfg"),
        P(),
        P("cfg", ("seq", "head"), None),
        P("head", None),
        P(),
        P("cfg", None),
        P("cfg", None),
        P(),
        P("cfg", ("seq", "head")),
        P(),
    )
    out_specs = (P("cfg", ("seq", "head")), P("cfg", ("seq", "head")))
    return jax.shard_map(shards, mesh=mesh, in_specs=in_specs, out_specs=out_specs, check_vma=False)
```

time: 204 us -> 122 us (0.60)
  waiting for transfers between devices: 52.9 us -> 0 us
  between operations: 15.6 us -> 1.93 us
  matrix products: 7.68 us -> 0 us
  Pallas kernels: 119 us -> 115 us
  starting transfers between devices: 3.27 us -> 0 us
    all_gather x1 -> x0, waiting for transfers between devices: 50.3 us -> none  [shards(): lax.all_gather(out_weight, 'head', axis=0, tiled=True)]
    dot_general x2 -> x0, matrix products: 7.68 us -> none  [the longest x1 6.63 us: shards(): lax.dot_general(attended, lax.all_gather(out_weight, 'head', axis=0, tile...]
    pallas_call x1, Pallas kernels: 119 us -> 115 us  [shards(): pl.pallas_call(block_kernel, out_shape=(out, out), in_specs=[anywhere] *...]
    all_to_all x1 -> x0, starting transfers between devices: 3.24 us -> none  [shards(): lax.all_to_all(halves.astype(jnp.bfloat16), 'cfg', split_axis=0, concat_a...]
  transfers between devices with their start and end apart: 2 -> 0, of which waited for: 2 -> 0; matrix products, arithmetic and copies ran while one was open for 0% -> 0% of each run, Pallas kernels for 59% -> 0%
where the time goes in v1:
time: 122 us; the launch traced here: 120 us
  Pallas kernels  115 us (94%)
  local copies, waits for them, and re-layouts  3.94 us (3%)
  between operations  1.93 us (2%)
    pallas_call x1, Pallas kernels, shards(): pl.pallas_call(block_kernel, out_shape=(out, out), in_specs=[anywhere] *...  115 us
    unnamed x2, local copies, waits for them, and re-layouts  2.65 us

profile of v1, /device:TPU:1, one launch (start us, length us, event | category | flops | bytes accessed | tf_op | source)
XLA Modules:
  0.0 120.4 jit_solution(15623355473958988356)
XLA Ops:
  1.9 1.3 %broadcast_in_dim.3.out_bias = bf16[1,2432]{1,0:T(2,128)(2,1)} reshape(bf16[2432]{0:T(1024)(128)(2,1)} %param.24) | data formatting | bytes 9728 | tf_op jit(solution)/shard_map/broadcast_in_dim | solution.py:682
  3.2 114.5 %shard_map.158 = (f32[32,128]{1,0:T(8,128)}, f32[32,128]{1,0:T(8,128)}) custom-call(bf16[1,128,2560]{2,1,0:T(8,128)(2,1)} %q_hbm.1, bf16[1,128,2560]{2,1,0:T(8,128)(2,1)} %k_hbm.1, bf16[1,128,2560]{2,1,0:T(8,128)(2,1)} %v_hbm.1, bf16[1,384,2560]{2,1,0:T(8,128)(2,1)} %tk_hbm.1, bf16[1,384,2560]{2,1,0:T(8,128)(2,1)} %tv_hbm.1, bf16[320,2432]{1,0:T(8,128)(2,1)} %w_hbm.1, ...), custom_call_target="tpu_custom_call" | custom-call | flops 40000000000 | bytes 20000000 | tf_op jit(solution)/shard_map/pallas_call | solution.py:623
  117.8 1.3 %copy.21 = f32[32,128]{1,0:T(8,128)} copy(f32[32,128]{1,0:T(8,128)} %get-tuple-element.4) | data formatting | bytes 32768
  119.1 1.3 %copy.22 = f32[32,128]{1,0:T(8,128)} copy(f32[32,128]{1,0:T(8,128)} %get-tuple-element.5) | data formatting | bytes 32768

commit v2 on v1

--- a/solution.py
+++ b/solution.py
@@ -35,16 +35,13 @@
     tv_hbm,
     w_hbm,
     hidden_hbm,
-    len_ref,
-    mask_ref,
-    step_ref,
-    out_bias,
-    shift_ref,
-    scale_ref,
-    final_weight,
-    latent_ref,
-    next_ref,
-    denoised_ref,
+    len_hbm,
+    mask_hbm,
+    bias_hbm,
+    shift_hbm,
+    scale_hbm,
+    final_hbm,
+    guided_ref,
     loaded,
     text_slab,
     q_stage,
@@ -68,6 +65,12 @@
     residual,
     v_stage,
     v_recv,
+    len_ref,
+    mask_ref,
+    out_bias,
+    shift_ref,
+    scale_ref,
+    final_weight,
     load_sem,
     q_send,
     q_recv_sem,
@@ -116,6 +119,19 @@
             for i in range(2)
         ]
         + [pltpu.make_async_copy(hidden_hbm.at[0], hidden, load_sem.at[7])]
+        + [
+            pltpu.make_async_copy(src, dst, load_sem.at[8 + i])
+            for i, (src, dst) in enumerate(
+                (
+                    (bias_hbm, out_bias),
+                    (shift_hbm, shift_ref),
+                    (scale_hbm, scale_ref),
+                    (final_hbm, final_weight),
+                    (mask_hbm, mask_ref),
+                    (len_hbm, len_ref),
+                )
+            )
+        ]
     )
     for load in loads:
         load.start()
@@ -149,7 +165,7 @@
         peer = lax.rem(group + d, 8)
         return pltpu.make_async_remote_copy(
             src_ref=src.at[peer],
-            dst_ref=dst.at[d % 2, row],
+            dst_ref=dst.at[0 if isinstance(d, int) else 1, row],
             send_sem=send.at[d],
             recv_sem=recv.at[d],
             device_id={"head": peer},
@@ -163,9 +179,10 @@
         return head_copy(kv_stage, kv, a_send, a_recv, d)
 
     along = (2, 6, 4)
-    across = (1, 7, 3, 5)
+    across = [lax.rem(1 + 2 * k + 6 * parity, 8) for k in range(4)]
     for d in along:
         q_copy(d).start()
+    q_copy(across[0]).start()
     q_recv[0, pl.ds(row, 1)] = q_stage[pl.ds(group, 1)]
 
     loads[1].wait()
@@ -193,10 +210,7 @@
             ]
     for d in along:
         kv_copy(d).start()
-    for d in across:
-        q_copy(d).start()
-    for d in across:
-        kv_copy(d).start()
+    kv_copy(across[0]).start()
     kv[0, pl.ds(row, 1)] = kv_stage[pl.ds(group, 1)]
 
     loads[3].wait()
@@ -244,8 +258,11 @@
             m_ref[GROUP_HEADS * t + h] = top
         return 0
 
+    loads[13].wait()
     for d in along:
         q_copy(d).wait_recv()
+    for d in across[1:]:
+        q_copy(d).start()
     lax.fori_loop(0, 2, queries_and_text, 0)
 
     def ring_copy(k, src, dst, target):
@@ -304,12 +321,12 @@
             weight_copy(1, group, to_left, True),
             weight_copy(2, group, to_turned, True),
         ),
-        1: (
-            weight_copy(3, lax.rem(group + 6 + 4 * core, 8), {"head": w_far}),
+        1: (weight_copy(3, lax.rem(group + 6 + 4 * core, 8), {"head": w_far}),),
+        2: (
+            weight_copy(6, w_opposite, to_turned),
             weight_copy(4, turned, to_right),
             weight_copy(5, turned, to_left),
         ),
-        2: (weight_copy(6, w_opposite, to_turned),),
     }
     to_core = [weight_copy(7 + k, owners[k], to_sibling) for k in range(7)]
 
@@ -328,18 +345,18 @@
     s_bufs = (s0, s1)
     p_bufs = (p0, p1)
 
-    def scores(step, r, t, h, buf):
-        best = None
+    def score_parts(step, r, t, h, buf):
         for side in range(2):
             slot = step[side]
             if h < 4:
-                lhs = jnp.concatenate(
-                    [kv[slot, b, 128 * (h // 2) : 128 * (h // 2 + 1), :] for b in range(4)], 0
-                )
-                s = jnp.dot(lhs, qx[6 * t + h], preferred_element_type=f32)
-                buf[512 * side : 512 * (side + 1), :] = s
-                top = jnp.max(s.reshape(64, 8, TILE), axis=0)
-                best = top if best is None else jnp.maximum(best, top)
+                for first in range(0, 4, 2):
+                    lhs = jnp.concatenate(
+                        [kv[slot, b, 128 * (h // 2) : 128 * (h // 2 + 1), :] for b in range(first, first + 2)], 0
+                    )
+                    s = jnp.dot(lhs, qx[6 * t + h], preferred_element_type=f32)
+                    at = 512 * side + 128 * first
+                    buf[at : at + 128 * 2, :] = s
+                    yield jnp.max(s.reshape(16 * 2, 8, TILE), axis=0)
             else:
                 lhs = jnp.concatenate([kv[slot, b, 256:320, :] for b in range(4)], 0)
                 for half in range(2):
@@ -347,31 +364,42 @@
                     for b in range(4):
                         at = 512 * side + 128 * b + HDIM * half
                         buf[at : at + HDIM, :] = s[HDIM * b : HDIM * (b + 1)]
-                    top = jnp.max(s.reshape(32, 8, TILE), axis=0)
-                    best = top if best is None else jnp.maximum(best, top)
+                    yield jnp.max(s.reshape(32, 8, TILE), axis=0)
+
+    def weigh_parts(buf, top, out):
+        for j in range(0, QUERIES, 256):
+            out[j : j + 256, :] = jnp.exp2((buf[j : j + 256, :] - top) * SCORE_SCALE).astype(bf16)
+            yield None
+
+    def value_parts(step, r, h, buf):
+        for side in range(2):
+            slot = step[side]
+            rows = FEATURES + HDIM * h
+            lhs = jnp.concatenate([kv[slot, b, rows : rows + HDIM, :] for b in range(4)], 1)
+            yield jnp.dot(
+                jnp.concatenate([lhs, ones], 0),
+                buf[512 * side : 512 * (side + 1), :],
+                preferred_element_type=f32,
+            )
+
+    def woven(*streams):
+        given = [[] for _ in streams]
+        waiting = [list_of for list_of in streams]
+        live = list(range(len(streams)))
+        while live:
+            for i in tuple(live):
+                try:
+                    given[i].append(next(waiting[i]))
+                except StopIteration:
+                    live.remove(i)
+        return given
+
+    def new_top(r, parts):
+        best = functools.reduce(jnp.maximum, parts)
         old = m_ref[r]
         new = jnp.maximum(old, jnp.max(best, axis=0, keepdims=True))
         m_ref[r] = new
         return new, jnp.exp2((old - new) * SCORE_SCALE)
-
-    def weigh(buf, top, out):
-        for j in range(4):
-            rows = slice(256 * j, 256 * (j + 1))
-            out[rows, :] = jnp.exp2((buf[rows, :] - top) * SCORE_SCALE).astype(bf16)
-
-    def add_values(step, r, h, rescale, buf):
-        total = None
-        for side in range(2):
-            slot = step[side]
-            rows = FEATURES + HDIM * h
-            lhs = jnp.concatenate([kv[slot, b, rows : rows + HDIM, :] for b in range(4)], 1)
-            part = jnp.dot(
-                jnp.concatenate([lhs, ones], 0),
-                buf[512 * side : 512 * (side + 1), :],
-                preferred_element_type=f32,
-            )
-            total = part if total is None else total + part
-        acc[r] = acc[r] * rescale + total
 
     def finish(t, _):
         for h in range(GROUP_HEADS):
@@ -387,7 +415,7 @@
     def o_copy(d):
         peer = lax.rem(group + d, 8)
         return pltpu.make_async_remote_copy(
-            src_ref=o_stage.at[d % 2, peer // 2],
+            src_ref=o_stage.at[0 if isinstance(d, int) else 1, peer // 2],
             dst_ref=o_recv.at[group],
             send_sem=o_send.at[d],
             recv_sem=o_recv_sem.at[d],
@@ -400,6 +428,8 @@
         def _():
             for d in along:
                 kv_copy(d).wait_recv()
+            for d in across[1:]:
+                kv_copy(d).start()
             send(0)
             arrived(2)
 
@@ -417,7 +447,7 @@
             weight_send(0)
             arrived(3)
 
-        @pl.when(half == 4)
+        @pl.when(half == 3)
         def _():
             arrived(4, 5)
             send(2)
@@ -430,20 +460,20 @@
         def _():
             arrived(12)
             send(4)
-
-        @pl.when(half == 8)
-        def _():
-            arrived(13)
             weight_arrived(0, 1, 2)
             weight_send(1)
             share(0, 1, 2)
 
-        @pl.when(half == 10)
+        @pl.when(half == 8)
+        def _():
+            arrived(13)
+
+        @pl.when(half == 9)
         def _():
             arrived(8, 9)
             send(3)
 
-        @pl.when(half == 11)
+        @pl.when(half == 10)
         def _():
             weight_arrived(3)
             weight_send(2)
@@ -464,9 +494,12 @@
 
         @pl.when(half == 15)
         def _():
+            loads[12].wait()
             lax.fori_loop(2, 4, finish, 0)
             for d in across:
                 o_copy(d).start()
+            weight_arrived(4, 5, 6)
+            share(4, 5, 6)
 
     def half_step(half, _):
         at_start(half)
@@ -486,18 +519,25 @@
         def unit(j):
             return 10 * side + j, 2 * side + j // 5, j % 5
 
-        top, rescale = scores(where, *unit(0), s0)
+        (parts,) = woven(score_parts(where, *unit(0), s0))
+        top, rescale = new_top(unit(0)[0], parts)
         before = None
         for j in range(10):
+            streams = [weigh_parts(s_bufs[j % 2], top, p_bufs[j % 2])]
+            if j < 9:
+                streams.insert(0, score_parts(where, *unit(j + 1), s_bufs[(j + 1) % 2]))
             if j > 0:
-                r, t, h = unit(j - 1)
-                add_values(where, r, h, before, p_bufs[(j + 1) % 2])
-            weigh(s_bufs[j % 2], top, p_bufs[j % 2])
+                r, _, h = unit(j - 1)
+                streams.append(value_parts(where, r, h, p_bufs[(j + 1) % 2]))
+            given = woven(*streams)
+            if j > 0:
+                acc[r] = acc[r] * before + functools.reduce(jnp.add, given[-1])
             before = rescale
             if j < 9:
-                top, rescale = scores(where, *unit(j + 1), s_bufs[(j + 1) % 2])
-        r, t, h = unit(9)
-        add_values(where, r, h, before, p1)
+                top, rescale = new_top(unit(j + 1)[0], given[0])
+        r, _, h = unit(9)
+        (given,) = woven(value_parts(where, r, h, p1))
+        acc[r] = acc[r] * before + functools.reduce(jnp.add, given)
         return 0
 
     lax.fori_loop(0, 16, half_step, 0)
@@ -505,11 +545,9 @@
     lax.fori_loop(0, 2, finish, 0)
     for d in along:
         o_copy(d).start()
-    weight_arrived(4, 5, 6)
-    share(4, 5, 6)
     o_recv[pl.ds(group, 1)] = o_stage[0, pl.ds(row, 1)]
 
-    for d in along + across:
+    for d in (*along, *across):
         q_copy(d).wait_send()
         kv_copy(d).wait_send()
     for stage in copies.values():
@@ -519,7 +557,7 @@
         for copy in stage:
             copy.wait_send()
 
-    for d in across + along:
+    for d in (*across, *along):
         o_copy(d).wait_recv()
     for p in range(8):
         for h in range(GROUP_HEADS):
@@ -530,7 +568,7 @@
                 nxt = f + HDIM
                 hi = o_recv[nxt // FEATURES, nxt % FEATURES : nxt % FEATURES + HDIM, :]
                 attended[:, 128 * q : 128 * (q + 1)] = jnp.concatenate([lo, hi], 0).T
-    for load in loads[5:]:
+    for load in loads[5:12]:
         load.wait()
     weight_arrived(7, 8, 9, 10, 11, 12, 13)
     rows = attended[...]
@@ -543,7 +581,7 @@
             jnp.concatenate([weight[i, :, cols] for i in range(16)], 0),
             preferred_element_type=f32,
         )
-        part = hidden[:, cols].astype(f32) + part + out_bias[:, cols].astype(f32)
+        part = hidden[:, cols].astype(f32) + part + out_bias[cols].astype(f32).reshape(1, -1)
         residual[:, cols] = part
         part = jnp.sum(part, axis=1, keepdims=True)
         total = part if total is None else total + part
@@ -581,10 +619,7 @@
     )
     exchange.start()
     mine = jnp.where(cfg == 0, velocity[:32], velocity[32:])
-    position = jnp.full((32, TOKENS), step_ref[0], jnp.int32)
-    sigma_now = sigma_at(position)
-    sigma_next = sigma_at(position + 1)
-    for d in along + across:
+    for d in (*along, *across):
         o_copy(d).wait_send()
     for copy in to_core:
         copy.wait_send()
@@ -592,9 +627,7 @@
     theirs = v_recv[...].astype(f32)
     cond = jnp.where(cfg == 0, mine, theirs)
     uncond = jnp.where(cfg == 0, theirs, mine)
-    guided = uncond + GUIDANCE * (cond - uncond)
-    denoised_ref[...] = latent_ref[...] - sigma_now * guided
-    next_ref[...] = latent_ref[...] + (sigma_next - sigma_now) * guided
+    guided_ref[...] = uncond + GUIDANCE * (cond - uncond)
 
 
 def shards(
@@ -617,14 +650,12 @@
     vmem = pltpu.VMEM
     dma = pltpu.SemaphoreType.DMA
     anywhere = pl.BlockSpec(memory_space=pl.ANY)
-    scalars = pl.BlockSpec(memory_space=pltpu.SMEM)
     whole = pl.BlockSpec(memory_space=pltpu.VMEM)
-    out = jax.ShapeDtypeStruct(latent.shape, f32)
-    return pl.pallas_call(
+    guided = pl.pallas_call(
         block_kernel,
-        out_shape=(out, out),
-        in_specs=[anywhere] * 7 + [scalars] * 3 + [whole] * 5,
-        out_specs=(whole, whole),
+        out_shape=jax.ShapeDtypeStruct(latent.shape, f32),
+        in_specs=[anywhere] * 13,
+        out_specs=whole,
         scratch_shapes=[
             vmem((3, TOKENS, 2560), bf16),
             vmem((2, SLOTS, 384), bf16),
@@ -649,7 +680,13 @@
             vmem((TOKENS, 2432), f32),
             vmem((2, 32, TOKENS), bf16),
             vmem((32, TOKENS), bf16),
-            dma((8,)),
+            pltpu.SMEM((1,), jnp.int32),
+            pltpu.SMEM((40,), jnp.int32),
+            vmem((2432,), bf16),
+            vmem((1, 2432), bf16),
+            vmem((1, 2432), bf16),
+            vmem((64, 2432), bf16),
+            dma((14,)),
             dma((8,)),
             dma((8,)),
             dma((8,)),
@@ -678,13 +715,16 @@
         hidden,
         text_len,
         head_mask,
-        step_index,
-        out_bias[None],
+        out_bias,
         final_shift,
         final_scale,
         final_weight,
-        latent,
     )
+    sigma_now = sigma_at(step_index[0])
+    sigma_next = sigma_at(step_index[0] + 1)
+    denoised = latent - sigma_now * guided
+    next_latent = latent + (sigma_next - sigma_now) * guided
+    return (next_latent, denoised)
 
 
 def solution(mesh):

time: 122 us -> 111 us (0.910)
  the two profiles are of different devices: /device:TPU:1 before, /device:TPU:39 now
where the time goes in v2:
time: 111 us
  Pallas kernels  108 us (97%)
  between operations  2.04 us (2%)
  other arithmetic  1.34 us (1%)
    pallas_call x1, Pallas kernels, shards(): pl.pallas_call(block_kernel, out_shape=jax.ShapeDtypeStruct(latent.shape,...  108 us

profile of v2, /device:TPU:39, one launch (start us, length us, event | category | flops | bytes accessed | tf_op | source)
XLA Modules:
  0.0 110.9 jit_solution(10978836436285477112)
XLA Ops:
  2.0 0.0 copy-start
  2.0 107.5 %shard_map.158 = f32[32,128]{1,0:T(8,128)} custom-call(bf16[1,128,2560]{2,1,0:T(8,128)(2,1)} %q_hbm.1, bf16[1,128,2560]{2,1,0:T(8,128)(2,1)} %k_hbm.1, bf16[1,128,2560]{2,1,0:T(8,128)(2,1)} %v_hbm.1, bf16[1,384,2560]{2,1,0:T(8,128)(2,1)} %tk_hbm.1, bf16[1,384,2560]{2,1,0:T(8,128)(2,1)} %tv_hbm.1, bf16[320,2432]{1,0:T(8,128)(2,1)} %w_hbm.1, ...), custom_call_target="tpu_custom_call" | custom-call | flops 40000000000 | bytes 20000000 | tf_op jit(solution)/shard_map/pallas_call | solution.py:654
  109.6 0.0 copy-done
  109.6 1.3 %multiply_subtract_fusion = (f32[32,128]{1,0:T(8,128)}, f32[32,128]{1,0:T(8,128)}) fusion(f32[32,128]{1,0:T(8,128)S(1)} %copy-done, f32[32,128]{1,0:T(8,128)} %shard_map.158, f32[]{:T(128)} %bitcast.1, f32[]{:T(128)S(6)} %sub.19), kind=kLoop, calls=%fused_computation | loop fusion | flops 16384 | bytes 65544 | tf_op jit(solution)/shard_map/sub | solution.py:725
Async XLA Ops:
  2.0 107.5 %copy-start = (f32[32,128]{1,0:T(8,128)S(1)}, f32[32,128]{1,0:T(8,128)}, u32[]{:S(2)}) copy-start(f32[32,128]{1,0:T(8,128)} %param.28) | copy-start | bytes 49156

commit v3 on v2

--- a/solution.py
+++ b/solution.py
@@ -78,6 +78,8 @@
     a_recv,
     b_send,
     b_recv,
+    c_send,
+    c_recv,
     o_send,
     o_recv_sem,
     w_send,
@@ -213,6 +215,20 @@
     kv_copy(across[0]).start()
     kv[0, pl.ds(row, 1)] = kv_stage[pl.ds(group, 1)]
 
+    def block_copy(k, d):
+        at = lax.rem(group + 8 - d, 8) // 2
+        return pltpu.make_async_remote_copy(
+            src_ref=kv.at[k // 4, at],
+            dst_ref=kv.at[2 + k // 4, at],
+            send_sem=c_send.at[k],
+            recv_sem=c_recv.at[k],
+            device_id={"seq": sibling},
+            device_id_type=MESH,
+        )
+
+    blocks = [block_copy(k, d) for k, d in enumerate((0, *along, *across))]
+    blocks[0].start()
+
     loads[3].wait()
     loads[4].wait()
     odd = parity == 1
@@ -276,12 +292,12 @@
         )
 
     copies = {
-        0: (ring_copy(2, 0, 2, sibling), ring_copy(0, 0, 4, right), ring_copy(1, 0, 5, left)),
-        1: (ring_copy(5, 1, 3, sibling), ring_copy(3, 1, 8, right), ring_copy(4, 1, 9, left)),
-        2: (ring_copy(6, 4 + core, 12, far), ring_copy(7, 4, 6, sibling), ring_copy(8, 5, 7, sibling)),
-        3: (ring_copy(9, 8 + core, 14, far), ring_copy(10, 8, 10, sibling), ring_copy(11, 9, 11, sibling)),
-        4: (ring_copy(12, 12, 13, sibling),),
-        5: (ring_copy(13, 14, 15, sibling),),
+        0: (ring_copy(0, 0, 4, right), ring_copy(1, 0, 5, left)),
+        1: (ring_copy(2, 1, 8, right), ring_copy(3, 1, 9, left)),
+        2: (ring_copy(4, 4, 6, sibling), ring_copy(5, 5, 7, sibling)),
+        3: (ring_copy(6, 4 + core, 12, far),),
+        4: (ring_copy(7, 8 + core, 14, far), ring_copy(8, 8, 10, sibling), ring_copy(9, 9, 11, sibling)),
+        5: (ring_copy(10, 12, 13, sibling), ring_copy(11, 14, 15, sibling)),
     }
 
     def arrived(*slots):
@@ -426,12 +442,14 @@
     def at_start(half):
         @pl.when(half == 0)
         def _():
-            for d in along:
+            for k, d in enumerate(along):
                 kv_copy(d).wait_recv()
+                blocks[1 + k].start()
+            send(0)
             for d in across[1:]:
                 kv_copy(d).start()
-            send(0)
-            arrived(2)
+            for block in blocks[:4]:
+                block.wait_recv()
 
         @pl.when(half == 1)
         def _():
@@ -441,13 +459,15 @@
 
         @pl.when(half == 2)
         def _():
-            for d in across:
+            for k, d in enumerate(across):
                 kv_copy(d).wait_recv()
+                blocks[4 + k].start()
             send(1)
             weight_send(0)
-            arrived(3)
-
-        @pl.when(half == 3)
+            for block in blocks[4:]:
+                block.wait_recv()
+
+        @pl.when(half == 4)
         def _():
             arrived(4, 5)
             send(2)
@@ -455,42 +475,34 @@
         @pl.when(half == 6)
         def _():
             arrived(6, 7)
+            send(3)
 
         @pl.when(half == 7)
         def _():
-            arrived(12)
-            send(4)
             weight_arrived(0, 1, 2)
             weight_send(1)
             share(0, 1, 2)
 
         @pl.when(half == 8)
         def _():
-            arrived(13)
-
-        @pl.when(half == 9)
-        def _():
             arrived(8, 9)
-            send(3)
+            send(4)
 
         @pl.when(half == 10)
         def _():
+            arrived(10, 11)
             weight_arrived(3)
             weight_send(2)
             share(3)
 
         @pl.when(half == 12)
         def _():
-            arrived(10, 11)
-
-        @pl.when(half == 13)
-        def _():
-            arrived(14)
+            arrived(12, 14)
             send(5)
 
         @pl.when(half == 14)
         def _():
-            arrived(15)
+            arrived(13, 15)
 
         @pl.when(half == 15)
         def _():
@@ -498,21 +510,12 @@
             lax.fori_loop(2, 4, finish, 0)
             for d in across:
                 o_copy(d).start()
-            weight_arrived(4, 5, 6)
-            share(4, 5, 6)
 
     def half_step(half, _):
         at_start(half)
         order = half // 2
-        slots = (
-            jnp.where(order == 0, 0, jnp.where(order == 1, 1, 0)),
-            jnp.where(order == 0, 2, jnp.where(order == 1, 3, 0)),
-        )
-        pair = jnp.where(
-            order < 4, order, jnp.where(order == 4, 6, jnp.where(order < 7, order - 1, 7))
-        )
-        one = jnp.where(order < 2, slots[0], 2 * pair)
-        two = jnp.where(order < 2, slots[1], 2 * pair + 1)
+        one = jnp.where(order < 2, order, jnp.where(order < 6, 2 * order, order + 6))
+        two = jnp.where(order < 2, order + 2, jnp.where(order < 6, 2 * order + 1, order + 8))
         side = jnp.where(order == 7, 1 - half % 2, half % 2)
         where = (one, two)
 
@@ -545,11 +548,15 @@
     lax.fori_loop(0, 2, finish, 0)
     for d in along:
         o_copy(d).start()
+    weight_arrived(4, 5, 6)
+    share(4, 5, 6)
     o_recv[pl.ds(group, 1)] = o_stage[0, pl.ds(row, 1)]
 
     for d in (*along, *across):
         q_copy(d).wait_send()
         kv_copy(d).wait_send()
+    for block in blocks:
+        block.wait_send()
     for stage in copies.values():
         for copy in stage:
             copy.wait_send()
@@ -691,8 +698,10 @@
             dma((8,)),
             dma((8,)),
             dma((8,)),
-            dma((14,)),
+            dma((12,)),
             dma((16,)),
+            dma((8,)),
+            dma((8,)),
             dma((8,)),
             dma((8,)),
             dma((14,)),

time: 111 us -> 106 us (0.955)
  the two profiles are of different devices: /device:TPU:39 before, /device:TPU:1 now
where the time goes in v3:
time: 106 us; the launch traced here: 104 us
  Pallas kernels  101 us (95%)
  between operations  2.04 us (2%)
  other arithmetic  1.34 us (1%)
    pallas_call x1, Pallas kernels, shards(): pl.pallas_call(block_kernel, out_shape=jax.ShapeDtypeStruct(latent.shape,...  101 us

profile of v3, /device:TPU:1, one launch (start us, length us, event | category | flops | bytes accessed | tf_op | source)
XLA Modules:
  0.0 104.1 jit_solution(2968058145150464744)
XLA Ops:
  2.0 0.0 copy-start
  2.0 100.7 %shard_map.158 = f32[32,128]{1,0:T(8,128)} custom-call(bf16[1,128,2560]{2,1,0:T(8,128)(2,1)} %q_hbm.1, bf16[1,128,2560]{2,1,0:T(8,128)(2,1)} %k_hbm.1, bf16[1,128,2560]{2,1,0:T(8,128)(2,1)} %v_hbm.1, bf16[1,384,2560]{2,1,0:T(8,128)(2,1)} %tk_hbm.1, bf16[1,384,2560]{2,1,0:T(8,128)(2,1)} %tv_hbm.1, bf16[320,2432]{1,0:T(8,128)(2,1)} %w_hbm.1, ...), custom_call_target="tpu_custom_call" | custom-call | flops 40000000000 | bytes 20000000 | tf_op jit(solution)/shard_map/pallas_call | solution.py:661
  102.7 0.0 copy-done
  102.7 1.3 %multiply_subtract_fusion = (f32[32,128]{1,0:T(8,128)}, f32[32,128]{1,0:T(8,128)}) fusion(f32[32,128]{1,0:T(8,128)S(1)} %copy-done, f32[32,128]{1,0:T(8,128)} %shard_map.158, f32[]{:T(128)} %bitcast.1, f32[]{:T(128)S(6)} %sub.19), kind=kLoop, calls=%fused_computation | loop fusion | flops 16384 | bytes 65544 | tf_op jit(solution)/shard_map/sub | solution.py:734
Async XLA Ops:
  2.0 100.7 %copy-start = (f32[32,128]{1,0:T(8,128)S(1)}, f32[32,128]{1,0:T(8,128)}, u32[]{:S(2)}) copy-start(f32[32,128]{1,0:T(8,128)} %param.28) | copy-start | bytes 49156

commit v4 on v3

--- a/solution.py
+++ b/solution.py
@@ -184,7 +184,8 @@
     across = [lax.rem(1 + 2 * k + 6 * parity, 8) for k in range(4)]
     for d in along:
         q_copy(d).start()
-    q_copy(across[0]).start()
+    for d in across:
+        q_copy(d).start()
     q_recv[0, pl.ds(row, 1)] = q_stage[pl.ds(group, 1)]
 
     loads[1].wait()
@@ -277,8 +278,6 @@
     loads[13].wait()
     for d in along:
         q_copy(d).wait_recv()
-    for d in across[1:]:
-        q_copy(d).start()
     lax.fori_loop(0, 2, queries_and_text, 0)
 
     def ring_copy(k, src, dst, target):

time: 106 us -> 103 us (0.972); the launches traced: 104 us -> 103 us
  Pallas kernels: 101 us -> 99.6 us
where the time goes in v4:
time: 103 us
  Pallas kernels  99.6 us (97%)
  between operations  2.04 us (2%)
  other arithmetic  1.34 us (1%)
    pallas_call x1, Pallas kernels, shards(): pl.pallas_call(block_kernel, out_shape=jax.ShapeDtypeStruct(latent.shape,...  99.6 us

profile of v4, /device:TPU:1, one launch (start us, length us, event | category | flops | bytes accessed | tf_op | source)
XLA Modules:
  0.0 103.0 jit_solution(1490719097860845969)
XLA Ops:
  2.0 0.0 copy-start
  2.0 99.6 %shard_map.158 = f32[32,128]{1,0:T(8,128)} custom-call(bf16[1,128,2560]{2,1,0:T(8,128)(2,1)} %q_hbm.1, bf16[1,128,2560]{2,1,0:T(8,128)(2,1)} %k_hbm.1, bf16[1,128,2560]{2,1,0:T(8,128)(2,1)} %v_hbm.1, bf16[1,384,2560]{2,1,0:T(8,128)(2,1)} %tk_hbm.1, bf16[1,384,2560]{2,1,0:T(8,128)(2,1)} %tv_hbm.1, bf16[320,2432]{1,0:T(8,128)(2,1)} %w_hbm.1, ...), custom_call_target="tpu_custom_call" | custom-call | flops 40000000000 | bytes 20000000 | tf_op jit(solution)/shard_map/pallas_call | solution.py:660
  101.7 0.0 copy-done
  101.7 1.3 %multiply_subtract_fusion = (f32[32,128]{1,0:T(8,128)}, f32[32,128]{1,0:T(8,128)}) fusion(f32[32,128]{1,0:T(8,128)S(1)} %copy-done, f32[32,128]{1,0:T(8,128)} %shard_map.158, f32[]{:T(128)} %bitcast.1, f32[]{:T(128)S(6)} %sub.19), kind=kLoop, calls=%fused_computation | loop fusion | flops 16384 | bytes 65544 | tf_op jit(solution)/shard_map/sub | solution.py:733
Async XLA Ops:
  2.0 99.7 %copy-start = (f32[32,128]{1,0:T(8,128)S(1)}, f32[32,128]{1,0:T(8,128)}, u32[]{:S(2)}) copy-start(f32[32,128]{1,0:T(8,128)} %param.28) | copy-start | bytes 49156

commit v5 on v4

--- a/solution.py
+++ b/solution.py
@@ -276,9 +276,9 @@
         return 0
 
     loads[13].wait()
-    for d in along:
+    for d in (*along, *across):
         q_copy(d).wait_recv()
-    lax.fori_loop(0, 2, queries_and_text, 0)
+    lax.fori_loop(0, 4, queries_and_text, 0)
 
     def ring_copy(k, src, dst, target):
         return pltpu.make_async_remote_copy(
@@ -449,12 +449,6 @@
                 kv_copy(d).start()
             for block in blocks[:4]:
                 block.wait_recv()
-
-        @pl.when(half == 1)
-        def _():
-            for d in across:
-                q_copy(d).wait_recv()
-            lax.fori_loop(2, 4, queries_and_text, 0)
 
         @pl.when(half == 2)
         def _():

time: 103 us -> 103 us (level)
  no operation moved by 1% of the time
where the time goes in v5:
time: 103 us
  Pallas kernels  99.8 us (97%)
  between operations  2.04 us (2%)
  other arithmetic  1.34 us (1%)
    pallas_call x1, Pallas kernels, shards(): pl.pallas_call(block_kernel, out_shape=jax.ShapeDtypeStruct(latent.shape,...  99.8 us

profile of v5, /device:TPU:1, one launch (start us, length us, event | category | flops | bytes accessed | tf_op | source)
XLA Modules:
  0.0 103.2 jit_solution(8514984709496066822)
XLA Ops:
  2.0 0.0 copy-start
  2.0 99.8 %shard_map.158 = f32[32,128]{1,0:T(8,128)} custom-call(bf16[1,128,2560]{2,1,0:T(8,128)(2,1)} %q_hbm.1, bf16[1,128,2560]{2,1,0:T(8,128)(2,1)} %k_hbm.1, bf16[1,128,2560]{2,1,0:T(8,128)(2,1)} %v_hbm.1, bf16[1,384,2560]{2,1,0:T(8,128)(2,1)} %tk_hbm.1, bf16[1,384,2560]{2,1,0:T(8,128)(2,1)} %tv_hbm.1, bf16[320,2432]{1,0:T(8,128)(2,1)} %w_hbm.1, ...), custom_call_target="tpu_custom_call" | custom-call | flops 40000000000 | bytes 20000000 | tf_op jit(solution)/shard_map/pallas_call | solution.py:654
  101.8 0.0 copy-done
  101.8 1.3 %multiply_subtract_fusion = (f32[32,128]{1,0:T(8,128)}, f32[32,128]{1,0:T(8,128)}) fusion(f32[32,128]{1,0:T(8,128)S(1)} %copy-done, f32[32,128]{1,0:T(8,128)} %shard_map.158, f32[]{:T(128)} %bitcast.1, f32[]{:T(128)S(6)} %sub.19), kind=kLoop, calls=%fused_computation | loop fusion | flops 16384 | bytes 65544 | tf_op jit(solution)/shard_map/sub | solution.py:727
Async XLA Ops:
  2.0 99.8 %copy-start = (f32[32,128]{1,0:T(8,128)S(1)}, f32[32,128]{1,0:T(8,128)}, u32[]{:S(2)}) copy-start(f32[32,128]{1,0:T(8,128)} %param.28) | copy-start | bytes 49156

commit v6 on v4

--- a/solution.py
+++ b/solution.py
@@ -182,7 +182,7 @@
 
     along = (2, 6, 4)
     across = [lax.rem(1 + 2 * k + 6 * parity, 8) for k in range(4)]
-    for d in along:
+    for d in (4, 2, 6):
         q_copy(d).start()
     for d in across:
         q_copy(d).start()
@@ -211,7 +211,7 @@
             kv_stage[f // FEATURES, pl.ds(FEATURES + f % FEATURES, HDIM), :] = block[
                 HDIM * half : HDIM * (half + 1)
             ]
-    for d in along:
+    for d in (4, 2, 6):
         kv_copy(d).start()
     kv_copy(across[0]).start()
     kv[0, pl.ds(row, 1)] = kv_stage[pl.ds(group, 1)]

time: 103 us -> 105 us (1.019); the launches traced: 103 us -> 104 us
  no operation moved by 1% of the time
where the time goes in v6:
time: 105 us; the launch traced here: 104 us
  Pallas kernels  100 us (95%)
  between operations  2.04 us (2%)
  other arithmetic  1.34 us (1%)
    pallas_call x1, Pallas kernels, shards(): pl.pallas_call(block_kernel, out_shape=jax.ShapeDtypeStruct(latent.shape,...  100 us

profile of v6, /device:TPU:1, one launch (start us, length us, event | category | flops | bytes accessed | tf_op | source)
XLA Modules:
  0.0 103.9 jit_solution(9957584634470936175)
XLA Ops:
  2.0 0.0 copy-start
  2.0 100.5 %shard_map.158 = f32[32,128]{1,0:T(8,128)} custom-call(bf16[1,128,2560]{2,1,0:T(8,128)(2,1)} %q_hbm.1, bf16[1,128,2560]{2,1,0:T(8,128)(2,1)} %k_hbm.1, bf16[1,128,2560]{2,1,0:T(8,128)(2,1)} %v_hbm.1, bf16[1,384,2560]{2,1,0:T(8,128)(2,1)} %tk_hbm.1, bf16[1,384,2560]{2,1,0:T(8,128)(2,1)} %tv_hbm.1, bf16[320,2432]{1,0:T(8,128)(2,1)} %w_hbm.1, ...), custom_call_target="tpu_custom_call" | custom-call | flops 40000000000 | bytes 20000000 | tf_op jit(solution)/shard_map/pallas_call | solution.py:660
  102.5 0.0 copy-done
  102.5 1.3 %multiply_subtract_fusion = (f32[32,128]{1,0:T(8,128)}, f32[32,128]{1,0:T(8,128)}) fusion(f32[32,128]{1,0:T(8,128)S(1)} %copy-done, f32[32,128]{1,0:T(8,128)} %shard_map.158, f32[]{:T(128)} %bitcast.1, f32[]{:T(128)S(6)} %sub.19), kind=kLoop, calls=%fused_computation | loop fusion | flops 16384 | bytes 65544 | tf_op jit(solution)/shard_map/sub | solution.py:733
Async XLA Ops:
  2.0 100.5 %copy-start = (f32[32,128]{1,0:T(8,128)S(1)}, f32[32,128]{1,0:T(8,128)}, u32[]{:S(2)}) copy-start(f32[32,128]{1,0:T(8,128)} %param.28) | copy-start | bytes 49156
